TPU v7x, 512 devices: a whole 4x4x16 slice. The times are simulated.
512 devices in a mesh: dp: 4 (over x), section: 32 (over z, core), tensor: 4 (over y).
Axes of the slice: x: 4, y: 4, z: 16, core: 2. Of those that a mesh axis runs over, the one named last changes fastest.
Arguments:
- hidden: bfloat16 [512, 8192], P('dp', ('section', 'tensor'))
- weight: bfloat16 [8192, 65536], P('dp', ('section', 'tensor'))
- labels: int32 [512], P('dp'), may hold values from 0 to 65535
- counts: int32 [4, 65536], P('dp', ('section', 'tensor')), may hold values from 0 to 1023, as said below
Outputs:
- grad_weight: bfloat16 [8192, 65536], P('dp', ('section', 'tensor'))
- grad_hidden_t: bfloat16 [8192, 512], P(('dp', 'section', 'tensor'))
- loss: float32 [4], P('dp')
Inputs may be any that keep to these rules, and one draw needn't show every extreme that they name: counts of replica r lie in 0 to 256 * (r + 1) - 1, and each replica reaches its largest value at some entry.
All inputs are finite; a program needn't handle non-finite values.
Results may differ from a plain program's by a relative error of at most 0.006.
Values may be sent and summed in bfloat16 or wider, within the bound.
A program may use at most 64 MiB of HBM per device.

v0:
```python
import jax
import jax.numpy as jnp
from jax import lax
from jax.sharding import PartitionSpec as P


def body(hidden, weight, labels, counts):
    batch_rows = labels.shape[0]
    vocab_local = weight.shape[1]
    features = lax.all_gather(hidden, ("section", "tensor"), axis=1, tiled=True)
    replica_blocks = lax.all_to_all(features, "dp", split_axis=1, concat_axis=0, tiled=True)
    logits = jnp.dot(
        features,
        lax.all_gather(weight, "dp", axis=0, tiled=True),
        preferred_element_type=jnp.float32,
    )
    totals = lax.psum(counts, "dp")
    factor = lax.rsqrt(1.0 + totals[0].astype(jnp.float32))
    offset = lax.axis_index(("section", "tensor")) * vocab_local
    column_ids = lax.broadcasted_iota(jnp.int32, logits.shape, 1) + offset
    is_label = column_ids == labels[:, None]
    local_top = jnp.max(logits, axis=1)
    local_total = jnp.sum(jnp.exp(logits - local_top[:, None]), axis=1)
    local_target = jnp.sum(jnp.where(is_label, logits, 0.0), axis=1)
    local_weight = jnp.sum(jnp.where(is_label, factor[None, :], 0.0), axis=1)
    row_top = lax.pmax(local_top, ("section", "tensor"))
    rescaled = local_total * jnp.exp(local_top - row_top)
    row_total, target, token_weight = lax.psum(
        (rescaled, local_target, local_weight), ("section", "tensor")
    )
    scaled = token_weight / jnp.mean(token_weight)
    loss_value = jnp.sum(scaled * (jnp.log(row_total) + row_top - target)) / batch_rows
    softmax_rows = jnp.exp(logits - row_top[:, None]) / row_total[:, None]
    grad_logits = (scaled[:, None] * (softmax_rows - is_label.astype(jnp.float32))).astype(
        jnp.bfloat16
    )
    grad_all = lax.all_gather(grad_logits, "dp", axis=0, tiled=True)
    grad_weight = lax.dot_general(
        replica_blocks, grad_all, (((0,), (0,)), ((), ())), preferred_element_type=jnp.float32
    ).astype(jnp.bfloat16)
    grad_hidden_t = lax.psum_scatter(
        lax.dot_general(
            weight, grad_all, (((1,), (1,)), ((), ())), preferred_element_type=jnp.float32
        ),
        ("section", "tensor"),
        scatter_dimension=0,
        tiled=True,
    ).astype(jnp.bfloat16)
    return (grad_weight, grad_hidden_t, loss_value.reshape(1))


def solution(mesh):
    in_specs = (
        P("dp", ("section", "tensor")),
        P("dp", ("section", "tensor")),
        P("dp"),
        P("dp", ("section", "tensor")),
    )
    out_specs = (P("dp", ("section", "tensor")), P(("dp", "section", "tensor"), None), P("dp"))
    return jax.shard_map(body, mesh=mesh, in_specs=in_specs, out_specs=out_specs, check_vma=False)
```

profile of v0, /device:TPU:1, one launch (start us, length us, event | category | flops | bytes accessed | tf_op | source)
XLA Modules:
  0.0 1032.4 jit_solution(3165591086656319149)
XLA Ops:
  7.2 0.7 all-gather.3.cloned.1.call-update
  8.0 0.7 all-gather.5.cloned.1.call-update
  8.7 0.0 reduce-scatter.4.cloned.1.call-start
  8.7 7.7 psum.28
  16.5 140.2 %all-gather.3.cloned.1.call-done = bf16[128,8192]{0,1:T(8,128)(2,1)} async-done(((bf16[128,64]{0,1:T(8,128)(2,1)}), bf16[128,8192]{0,1:T(8,128)(2,1)}) %all-gather.3.cloned.1.call-update) | async-done | bytes 2097168 | tf_op jit(solution)/shard_map/all_gather | solution.py:10
  156.7 88.7 %all-gather.5.cloned.1.call-done = bf16[8192,512]{1,0:T(8,128)(2,1)} async-done(((bf16[2048,512]{1,0:T(8,128)(2,1)}), bf16[8192,512]{1,0:T(8,128)(2,1)}) %all-gather.5.cloned.1.call-update) | async-done | bytes 8388624 | tf_op jit(solution)/shard_map/all_gather | solution.py:14
  245.4 5.4 fusion.6
  250.8 248.1 %pmax.7 = f32[128]{0:T(128)S(1)} all-reduce(f32[128]{0:T(128)S(1)} %get-tuple-element.23), channel_id=1, replica_groups=mesh['dp'=4,'section'=32,'tensor'=4] {'section','tensor'}, use_global_device_ids=true, to_apply=%region_5.6 | all-reduce | flops 128 | bytes 1024 | tf_op jit(solution)/shard_map/pmax | solution.py:26
  498.9 0.2 fusion.5
  499.2 246.8 %all-reduce = (f32[128]{0:T(128)S(1)}, f32[128]{0:T(128)S(1)}, f32[128]{0:T(128)S(1)}) all-reduce(f32[128]{0:T(128)S(1)} %exponential_multiply_fusion, f32[128]{0:T(128)S(1)} %get-tuple-element.17, f32[128]{0:T(128)S(1)} %get-tuple-element.15), channel_id=1, replica_groups=mesh['dp'=4,'section'=32,'tensor'=4] {'section','tensor'}, use_global_device_ids=true, to_apply=%region_7.8 | all-reduce | flops 384 | bytes 3072 | tf_op jit(solution)/shard_map/psum | solution.py:28
  746.0 0.6 reduce_sum.46
  747.3 0.6 multiply_reduce_fusion
  747.9 0.1 fusion.4
  748.0 10.3 %all_gather.11 = bf16[512,512]{1,0:T(8,128)(2,1)S(1)} all-gather(bf16[128,512]{1,0:T(8,128)(2,1)S(1)} %fusion.4), channel_id=1, replica_groups=mesh['dp'=4,'section'=32,'tensor'=4] {'dp'}, dimensions={0}, use_global_device_ids=true | all-gather | bytes 655360 | tf_op jit(solution)/shard_map/all_gather | solution.py:37
  758.4 3.3 convolution_bitcast_fusion
  761.6 5.3 copy.17
  767.0 1.6 copy-done
  768.6 21.7 %all_to_all.19 = bf16[128,4,2048]{0,2,1:T(8,128)(2,1)} all-to-all(bf16[128,4,2048]{0,2,1:T(8,128)(2,1)S(1)} %bitcast.16), channel_id=1, replica_groups=mesh['dp'=4,'section'=32,'tensor'=4] {'dp'}, dimensions={1} | all-to-all | bytes 4194304 | tf_op jit(solution)/shard_map/all_to_all | solution.py:11
  790.2 2.9 copy.14
  793.2 2.6 fusion
  795.8 4.0 copy.15
  800.4 222.7 %reduce-scatter.4.cloned.1.call-done = f32[16,512]{1,0:T(8,128)} async-done(((f32[2048,512]{1,0:T(8,128)}), f32[16,512]{1,0:T(8,128)}) %reduce-scatter.4.cloned.1.call-update) | async-done | bytes 32784
  1023.1 0.9 copy.18
  1024.0 0.7 copy.16
  (13 shorter events, 0.1 us)
Async XLA Ops:
  7.2 1.5 copy-start.3
  7.2 149.5 %all-gather.3.cloned.1.call-start = ((), (), s32[]{:S(2)}) async-start(), calls=%async_computation.2 | async-start | bytes 2113536 | tf_op jit(solution)/shard_map/all_gather | solution.py:10
  7.9 237.5 %all-gather.5.cloned.1.call-start = ((), (), s32[]{:S(2)}) async-start(), calls=%async_computation.3 | async-start | bytes 10485760 | tf_op jit(solution)/shard_map/all_gather | solution.py:14
  8.7 1014.5 %reduce-scatter.4.cloned.1.call-start = ((), (), s32[]{:S(2)}) async-start(), calls=%async_computation.4 | async-start | bytes 4227072
  16.5 482.5 %copy-start.2 = (s32[128]{0:T(128)S(1)}, s32[128]{0:T(128)}, u32[]{:S(2)}) copy-start(s32[128]{0:T(128)} %param.6) | copy-start | bytes 1540
  16.5 741.9 %copy-start.1 = (bf16[2048,512]{1,0:T(8,128)(2,1)S(1)}, bf16[2048,512]{1,0:T(8,128)(2,1)}, u32[]{:S(2)}) copy-start(bf16[2048,512]{1,0:T(8,128)(2,1)} %param.5) | copy-start | bytes 6291460
  767.0 1.6 copy-start
Sparse Core Ops, SparseCore 0:
  11.1 145.4 all-gather.2
  158.8 86.5 all-gather.4
  767.1 255.9 reduce-scatter.3
where the time goes:
time: 1040 us; the launch traced here: 1030 us
  blocking collectives  535 us (51%)
  waiting for transfers between devices  453 us (44%)
  between operations  16.3 us (2%)
  local copies, waits for them, and re-layouts  15.4 us (1%)
  matrix products  11.3 us (1%)
    pmax x1, blocking collectives, body(): row_top = lax.pmax(local_top, ('section', 'tensor'))  248 us
    psum x1, blocking collectives, body(): lax.psum((rescaled, local_target, local_weight), ('section', 'tensor'))  247 us
    unnamed x4, waiting for transfers between devices  224 us
    all_gather x1, waiting for transfers between devices, body(): features = lax.all_gather(hidden, ('section', 'tensor'), axis=1, tiled=True)  140 us
    all_gather x1, waiting for transfers between devices, body(): lax.all_gather(weight, 'dp', axis=0, tiled=True)  88.7 us
    all_to_all x1, blocking collectives, body(): lax.all_to_all(features, 'dp', split_axis=1, concat_axis=0, tiled=True)  21.7 us
  transfers between devices with their start and end apart: 3, of which 3 were waited for; matrix products, arithmetic and copies ran while one was open for 1% of the time, Pallas kernels for 0%

commit v1 on v0

v1 whole, which is shorter than its diff:
```python
import functools

import jax
import jax.numpy as jnp
from jax import lax
from jax.experimental import pallas as pl
from jax.experimental.pallas import tpu as pltpu
from jax.sharding import PartitionSpec as P

NX, NY, NZ, NC = 4, 4, 16, 2
ZL = NZ // NX
BATCH = 128
FEAT = 64
VL = 512
MESH = pl.DeviceIdType.MESH
BF = jnp.bfloat16
F32 = jnp.float32


def spread(i):
    half = (i + 1) // 2
    return NZ // 2 + (1 - 2 * lax.rem(i, 2)) * half


def kernel(
    hid, w_hbm, lab, cnt,
    gw_hbm, gh_out, loss_out,
    wv, wt, zbuf, ht, part, bufa, bufb, rfl, rfr, cbuf, fcol, ebuf, stz, sty, gt,
    psend, pown, crecv, q, ya, yb, sa, sb, yl, yr, rz, zrb, gwv,
    w_sem, gw_sem,
    az_s, az_r, ax_s, ax_r, ct_s, ct_r, ay_s, ay_r, ac_s, ac_r,
    b_s, b_r, sz_s, sz_r, sy_s, sy_r, d_s, d_r,
    fc_s, fc_r, fy_s, fy_r, fz_s, fz_r,
):
    x = lax.axis_index("dp")
    s = lax.axis_index("section")
    y = lax.axis_index("tensor")
    z, c = s // 2, lax.rem(s, 2)
    zs, zl0 = z // ZL, lax.rem(z, ZL)
    oc = 1 - c

    def xat(k):
        return lax.rem(x + k + NX, NX)

    def yat(k):
        return lax.rem(y + k + NY, NY)

    def zat(k):
        return lax.rem(z + k + NZ, NZ)

    def to_x(k):
        return (xat(k), s, y)

    def to_y(k):
        return (x, s, yat(k))

    def to_z(zz):
        return (x, 2 * zz + c, y)

    def to_q(k):
        j = lax.rem(y * 2 + c + k, 8)
        return (x, 2 * z + lax.rem(j, 2), j // 2)

    sibling = (x, 2 * z + oc, y)
    sends = []

    def rcopy(src, dst, ss, rs, dev):
        return pltpu.make_async_remote_copy(
            src_ref=src, dst_ref=dst, send_sem=ss, recv_sem=rs, device_id=dev, device_id_type=MESH
        )

    def send(src, dst, ss, rs, dev):
        d = rcopy(src, dst, ss, rs, dev)
        d.start()
        sends.append(d)

    def recv(dst, rs):
        rcopy(dst, dst, rs, rs, sibling).wait_recv()

    w_copy = pltpu.make_async_copy(w_hbm, wv, w_sem)
    w_copy.start()

    eye = (lax.broadcasted_iota(jnp.int32, (FEAT, FEAT), 0) == lax.broadcasted_iota(jnp.int32, (FEAT, FEAT), 1))
    zbuf[z] = lax.dot_general(
        eye.astype(F32).astype(BF), hid[...], (((1,), (1,)), ((), ())), preferred_element_type=F32
    ).astype(BF)
    cbuf[x] = cnt[...]

    barrier = pltpu.get_barrier_semaphore()

    def greet_z(k, _):
        pl.semaphore_signal(barrier, inc=1, device_id=to_z(zat(k)), device_id_type=MESH)
        return 0

    lax.fori_loop(1, NZ, greet_z, 0)
    for k in range(1, 8):
        pl.semaphore_signal(barrier, inc=1, device_id=to_q(k), device_id_type=MESH)
    for k in range(1, NX):
        pl.semaphore_signal(barrier, inc=1, device_id=to_x(k), device_id_type=MESH)
    pl.semaphore_wait(barrier, 25)

    def start_z(i, _):
        k = spread(i)
        rcopy(zbuf.at[z], zbuf.at[z], az_s.at[k], az_r.at[k], to_z(zat(k))).start()
        return 0

    lax.fori_loop(0, NZ - 1, start_z, 0)
    for k in range(1, NX):
        send(cbuf.at[x], cbuf.at[x], ct_s.at[k], ct_r.at[k], to_x(k))

    w_copy.wait()

    def turn(i, _):
        rows = wv[pl.ds(2 * i, 2)].reshape(256, VL)
        wt[:, pl.ds(pl.multiple_of(i * 256, 256), 256)] = rows.T
        return 0

    lax.fori_loop(0, 8, turn, 0)
    for k in range(1, NX):
        recv(cbuf.at[xat(-k)], ct_r.at[k])
    totals = cbuf[0] + cbuf[1] + cbuf[2] + cbuf[3]
    factor = lax.rsqrt(1.0 + totals.astype(F32))
    fcol[...] = jnp.broadcast_to(factor, (BATCH, VL)).T

    def wait_z(k, _):
        recv(zbuf.at[zat(-k)], az_r.at[k])
        return 0

    lax.fori_loop(1, NZ, wait_z, 0)

    for k in (2, 1, 3):
        to = xat(k)
        send(zbuf.at[pl.ds(ZL * to, ZL)], ht.at[x, :, c, y], ax_s.at[k], ax_r.at[k], to_x(k))
    ht[x, :, c, y] = zbuf[pl.ds(ZL * x, ZL)]

    def hid_y(k):
        r = xat(-k)
        if k:
            recv(ht.at[r, :, c, y], ax_r.at[k])
        for d, e in ((0, 1), (1, -1)):
            send(ht.at[r, :, c, y], ht.at[r, :, c, y], ay_s.at[k, d], ay_r.at[k, d], to_y(e))

    def hid_relay(k):
        r = xat(-k)
        for d, e in ((0, 1), (1, -1)):
            recv(ht.at[r, :, c, yat(-e)], ay_r.at[k, d])
            half = pl.ds(2 * d, 2)
            ref = ht.at[r, half, c, yat(-e)]
            send(ref, ref, ay_s.at[k, 2 + d], ay_r.at[k, 2 + d], to_y(e))

    def hid_core(k):
        r = xat(-k)
        for d in (0, 1):
            recv(ht.at[r, pl.ds(2 * d, 2), c, yat(2)], ay_r.at[k, 2 + d])
        send(ht.at[r, :, c], ht.at[r, :, c], ac_s.at[k], ac_r.at[k], sibling)

    def logits_of(k):
        r = xat(-k)
        recv(ht.at[r, :, oc], ac_r.at[k])

        def tile(i, _):
            rows = pl.ds(pl.multiple_of(i * 256, 256), 256)
            part[r, rows] = jnp.dot(wt[rows, :], ht[r].reshape(2048, BATCH), preferred_element_type=F32)
            return 0

        lax.fori_loop(0, 2, tile, 0)
        top, low = pl.ds(0, 256), pl.ds(256, 256)
        if k == 2:
            send(part.at[r, top], bufa, b_s.at[0], b_r.at[0], to_x(1))
            send(part.at[r, low], bufb, b_s.at[1], b_r.at[1], to_x(-1))
        if k == 3:
            send(part.at[r, low], rfl.at[low], b_s.at[2], b_r.at[2], to_x(1))
            recv(bufa, b_r.at[0])
            part[r, top] = part[r, top] + bufa[...]
            send(part.at[r, top], rfl.at[top], b_s.at[3], b_r.at[3], to_x(1))
        if k == 1:
            send(part.at[r, top], rfr.at[top], b_s.at[4], b_r.at[4], to_x(-1))
            recv(bufb, b_r.at[1])
            part[r, low] = part[r, low] + bufb[...]
            send(part.at[r, low], rfr.at[low], b_s.at[5], b_r.at[5], to_x(-1))

    stages = (hid_y, hid_relay, hid_core, logits_of)
    order = (2, 1, 3, 0)
    for t in range(len(order) + len(stages) - 1):
        for j, stage in enumerate(stages):
            if 0 <= t - j < len(order):
                stage(order[t - j])

    top, low = pl.ds(0, 256), pl.ds(256, 256)
    recv(rfl.at[low], b_r.at[2])
    recv(rfl.at[top], b_r.at[3])
    recv(rfr.at[top], b_r.at[4])
    recv(rfr.at[low], b_r.at[5])

    logits = part[x] + rfl[...] + rfr[...]
    ids = lax.broadcasted_iota(jnp.int32, (VL, BATCH), 0) + (s * NY + y) * VL
    hit = ids == lab[...]
    m0 = jnp.max(logits, axis=0, keepdims=True)
    e0 = jnp.exp(logits - m0)
    ebuf[...] = e0
    zero = jnp.zeros((4, BATCH), F32)
    stz[z] = jnp.concatenate(
        [
            m0,
            jnp.sum(e0, axis=0, keepdims=True),
            jnp.sum(jnp.where(hit, logits, 0.0), axis=0, keepdims=True),
            jnp.sum(jnp.where(hit, fcol[...], 0.0), axis=0, keepdims=True),
            zero,
        ],
        axis=0,
    )

    def combine(ref):
        v = ref[...]
        tops = v[:, 0:1, :]
        m = jnp.max(tops, axis=0)
        t = jnp.sum(v[:, 1:2, :] * jnp.exp(tops - m[None]), axis=0)
        return m, t, jnp.sum(v[:, 2:3, :], axis=0), jnp.sum(v[:, 3:4, :], axis=0)

    def start_sz(i, _):
        k = spread(i)
        rcopy(stz.at[z], stz.at[z], sz_s.at[k], sz_r.at[k], to_z(zat(k))).start()
        return 0

    def wait_sz(k, _):
        recv(stz.at[zat(-k)], sz_r.at[k])
        return 0

    lax.fori_loop(0, NZ - 1, start_sz, 0)
    lax.fori_loop(1, NZ, wait_sz, 0)
    me = y * 2 + c
    sty[me] = jnp.concatenate([*combine(stz), zero], axis=0)
    for k in range(1, 8):
        send(sty.at[me], sty.at[me], sy_s.at[k], sy_r.at[k], to_q(k))
    for k in range(1, 8):
        recv(sty.at[lax.rem(me - k + 8, 8)], sy_r.at[k])
    m, total, target, weight = combine(sty)
    scaled = weight / jnp.mean(weight)
    loss_out[0] = jnp.sum(scaled * (jnp.log(total) + m - target)) / BATCH
    rate = jnp.exp(m0 - m) / total
    gt[x] = (scaled * (ebuf[...] * rate - hit.astype(F32))).astype(BF)

    for d, e in ((0, 1), (1, -1)):
        send(gt.at[x], gt.at[x], d_s.at[d], d_r.at[d], to_x(e))
    for d, e in ((0, 1), (1, -1)):
        recv(gt.at[xat(-e)], d_r.at[d])
        ref = gt.at[xat(-e), pl.ds(256 * d, 256)]
        send(ref, ref, d_s.at[2 + d], d_r.at[2 + d], to_x(e))
    for d in (0, 1):
        recv(gt.at[xat(2), pl.ds(256 * d, 256)], d_r.at[2 + d])

    def gall():
        return jnp.concatenate([gt[r] for r in range(NX)], axis=1)

    def gh_dot(k):
        zz = lax.rem(zs + k, NX)
        rows = wv[pl.ds(ZL * zz, ZL), oc].reshape(256, VL)
        psend[zz] = jnp.dot(rows, gall(), preferred_element_type=F32).astype(BF).reshape(ZL, NY, 16, 512)
        send(psend.at[zz], crecv.at[zz], fc_s.at[k], fc_r.at[k], sibling)
        rows = wv[pl.ds(ZL * zz, ZL), c].reshape(256, VL)
        pown[zz] = jnp.dot(rows, gall(), preferred_element_type=F32).reshape(ZL, NY, 16, 512)

    def gh_core(k):
        zz = lax.rem(zs + k, NX)
        recv(crecv.at[zz], fc_r.at[k])
        q[zz] = (pown[zz] + crecv[zz].astype(F32)).astype(BF)
        up, down = pl.ds(0, 2), pl.ds(2, 2)
        send(q.at[zz, up, yat(2)], ya.at[k], fy_s.at[k, 0], fy_r.at[k, 0], to_y(1))
        send(q.at[zz, down, yat(2)], yb.at[k], fy_s.at[k, 1], fy_r.at[k, 1], to_y(-1))
        send(q.at[zz, down, yat(1)], yl.at[k, down], fy_s.at[k, 2], fy_r.at[k, 2], to_y(1))
        send(q.at[zz, up, yat(-1)], yr.at[k, up], fy_s.at[k, 3], fy_r.at[k, 3], to_y(-1))

    def gh_relay(k):
        zz = lax.rem(zs + k, NX)
        up, down = pl.ds(0, 2), pl.ds(2, 2)
        recv(ya.at[k], fy_r.at[k, 0])
        sa[k] = (q[zz, up, yat(1)].astype(F32) + ya[k].astype(F32)).astype(BF)
        send(sa.at[k], yl.at[k, up], fy_s.at[k, 4], fy_r.at[k, 4], to_y(1))
        recv(yb.at[k], fy_r.at[k, 1])
        sb[k] = (q[zz, down, yat(-1)].astype(F32) + yb[k].astype(F32)).astype(BF)
        send(sb.at[k], yr.at[k, down], fy_s.at[k, 5], fy_r.at[k, 5], to_y(-1))

    def gh_z(k):
        zz = lax.rem(zs + k, NX)
        up, down = pl.ds(0, 2), pl.ds(2, 2)
        recv(yl.at[k, down], fy_r.at[k, 2])
        recv(yr.at[k, up], fy_r.at[k, 3])
        recv(yl.at[k, up], fy_r.at[k, 4])
        recv(yr.at[k, down], fy_r.at[k, 5])
        rz[zz] = (q[zz, :, y].astype(F32) + yl[k].astype(F32) + yr[k].astype(F32)).astype(BF)
        for j in range(0 if k else 1, ZL):
            l = lax.rem(zl0 + j, ZL)
            send(rz.at[zz, l], zrb.at[z], fz_s.at[k, j], fz_r.at[z], to_z(ZL * zz + l))

    stages = (gh_dot, gh_core, gh_relay, gh_z)
    order = (2, 1, 3, 0)
    for t in range(len(order) + len(stages) - 1):
        for j, stage in enumerate(stages):
            if 0 <= t - j < len(order):
                stage(order[t - j])

    def gw_tile(i, _):
        lhs = jnp.concatenate([ht[r, i // 2, lax.rem(i, 2)].reshape(256, BATCH) for r in range(NX)], axis=1)
        gwv[i] = lax.dot_general(lhs, gall(), (((1,), (1,)), ((), ())), preferred_element_type=F32).astype(BF)
        pltpu.make_async_copy(gwv.at[i], gw_hbm.at[i], gw_sem.at[i]).start()
        return 0

    lax.fori_loop(0, 8, gw_tile, 0)

    zrb[z] = rz[zs, zl0]

    def wait_fz(k, _):
        recv(zrb.at[zat(-k)], fz_r.at[zat(-k)])
        return 0

    lax.fori_loop(1, NZ, wait_fz, 0)
    gh_out[...] = jnp.sum(zrb[...].astype(F32), axis=0).astype(BF)

    def gw_wait(i, _):
        pltpu.make_async_copy(gwv.at[i], gw_hbm.at[i], gw_sem.at[i]).wait()
        return 0

    lax.fori_loop(0, 8, gw_wait, 0)

    def done_z(k, _):
        rcopy(zbuf.at[z], zbuf.at[z], az_s.at[k], az_r.at[k], sibling).wait_send()
        rcopy(stz.at[z], stz.at[z], sz_s.at[k], sz_r.at[k], sibling).wait_send()
        return 0

    lax.fori_loop(1, NZ, done_z, 0)
    for d in sends:
        d.wait_send()


def body(hidden, weight, labels, counts):
    dma = pltpu.SemaphoreType.DMA
    v = pltpu.VMEM
    scratch = [
        v((16, 2, 64, VL), BF),
        v((VL, 2048), BF),
        v((NZ, FEAT, BATCH), BF),
        v((NX, ZL, NC, NY, FEAT, BATCH), BF),
        v((NX, VL, BATCH), F32),
        v((256, BATCH), F32),
        v((256, BATCH), F32),
        v((VL, BATCH), F32),
        v((VL, BATCH), F32),
        v((NX, 1, VL), jnp.int32),
        v((VL, BATCH), F32),
        v((VL, BATCH), F32),
        v((NZ, 8, BATCH), F32),
        v((8, 8, BATCH), F32),
        v((NX, VL, BATCH), BF),
        v((NX, ZL, NY, 16, 512), BF),
        v((NX, ZL, NY, 16, 512), F32),
        v((NX, ZL, NY, 16, 512), BF),
        v((NX, ZL, NY, 16, 512), BF),
        v((NX, 2, 16, 512), BF),
        v((NX, 2, 16, 512), BF),
        v((NX, 2, 16, 512), BF),
        v((NX, 2, 16, 512), BF),
        v((NX, ZL, 16, 512), BF),
        v((NX, ZL, 16, 512), BF),
        v((NX, ZL, 16, 512), BF),
        v((NZ, 16, 512), BF),
        v((8, 256, VL), BF),
        dma, dma((8,)),
        dma((16,)), dma((16,)), dma((4,)), dma((4,)), dma((4,)), dma((4,)),
        dma((4, 4)), dma((4, 4)), dma((4,)), dma((4,)),
        dma((6,)), dma((6,)), dma((16,)), dma((16,)), dma((8,)), dma((8,)), dma((4,)), dma((4,)),
        dma((4,)), dma((4,)), dma((4, 6)), dma((4, 6)), dma((4, 4)), dma((16,)),
    ]
    vmem = pl.BlockSpec(memory_space=pltpu.VMEM)
    hbm = pl.BlockSpec(memory_space=pl.ANY)
    gw, gh, loss = pl.pallas_call(
        kernel,
        out_shape=(
            jax.ShapeDtypeStruct((8, 256, VL), BF),
            jax.ShapeDtypeStruct((16, 512), BF),
            jax.ShapeDtypeStruct((1,), F32),
        ),
        in_specs=[vmem, hbm, vmem, vmem],
        out_specs=(hbm, vmem, pl.BlockSpec(memory_space=pltpu.SMEM)),
        scratch_shapes=scratch,
        compiler_params=pltpu.CompilerParams(
            collective_id=0, has_side_effects=True, vmem_limit_bytes=48 * 1024 * 1024
        ),
        cost_estimate=pl.CostEstimate(flops=3 * 2**30, bytes_accessed=2**22, transcendentals=2**16),
    )(hidden, weight.reshape(16, 2, 64, VL), labels.reshape(1, BATCH), counts)
    return gw.reshape(2048, VL), gh, loss


def solution(mesh):
    in_specs = (
        P("dp", ("section", "tensor")),
        P("dp", ("section", "tensor")),
        P("dp"),
        P("dp", ("section", "tensor")),
    )
    out_specs = (P("dp", ("section", "tensor")), P(("dp", "section", "tensor"), None), P("dp"))
    return jax.shard_map(body, mesh=mesh, in_specs=in_specs, out_specs=out_specs, check_vma=False)
```

time: 1040 us -> 112 us (0.11)
  blocking collectives: 535 us -> 0 us
  waiting for transfers between devices: 453 us -> 0 us
  Pallas kernels: 0 us -> 103 us
  between operations: 16.3 us -> 2.39 us
  matrix products: 11.3 us -> 0 us
    psum x2 -> x0, blocking collectives: 255 us -> none  [the longest x1 247 us: body(): lax.psum((rescaled, local_target, local_weight), ('section', 'tensor'))]
    pmax x1 -> x0, blocking collectives: 248 us -> none  [body(): row_top = lax.pmax(local_top, ('section', 'tensor'))]
    all_gather x2 -> x0, waiting for transfers between devices: 229 us -> none  [the longest x1 140 us: body(): features = lax.all_gather(hidden, ('section', 'tensor'), axis=1, tiled=True)]
    unnamed x4 -> x0, waiting for transfers between devices: 224 us -> none
    pallas_call x0 -> x1, Pallas kernels: none -> 103 us  [body(): pl.pallas_call(kernel, out_shape=(jax.ShapeDtypeStruct((8, 256, VL), BF),...]
    all_to_all x1 -> x0, blocking collectives: 21.7 us -> none  [body(): lax.all_to_all(features, 'dp', split_axis=1, concat_axis=0, tiled=True)]
    dot_general x3 -> x0, matrix products: 11.3 us -> none  [the longest x1 5.39 us: body(): jnp.dot(features, lax.all_gather(weight, 'dp', axis=0, tiled=True), prefe...]
  transfers between devices with their start and end apart: 3 -> 0, of which waited for: 3 -> 0; matrix products, arithmetic and copies ran while one was open for 1% -> 0% of each run, Pallas kernels for 0% -> 0%
where the time goes in v1:
time: 112 us; the launch traced here: 111 us
  Pallas kernels  103 us (92%)
  local copies, waits for them, and re-layouts  5.68 us (5%)
  between operations  2.39 us (2%)
    pallas_call x1, Pallas kernels, body(): pl.pallas_call(kernel, out_shape=(jax.ShapeDtypeStruct((8, 256, VL), BF),...  103 us
    unnamed x9, local copies, waits for them, and re-layouts  5.68 us

profile of v1, /device:TPU:1, one launch (start us, length us, event | category | flops | bytes accessed | tf_op | source)
XLA Modules:
  0.0 111.4 jit_solution(8415414070463995745)
XLA Ops:
  0.6 0.8 copy.7.hid
  1.5 0.0 copy-start
  1.5 1.6 %copy-done = bf16[2048,512]{1,0:T(8,128)(2,1)S(1)} copy-done((bf16[2048,512]{1,0:T(8,128)(2,1)S(1)}, bf16[2048,512]{1,0:T(8,128)(2,1)}, u32[]{:S(2)}) %copy-start) | copy-done | bytes 2097176
  3.1 0.0 copy-start.1
  3.1 0.7 copy-done.1
  3.7 0.0 copy-start.2
  3.7 0.7 copy-done.2
  4.4 103.4 %shard_map.67 = (bf16[8,256,512]{2,1,0:T(8,128)(2,1)S(1)}, bf16[16,512]{1,0:T(8,128)(2,1)S(1)}, f32[1]{0:T(128)}) custom-call(bf16[128,64]{1,0:T(8,128)(2,1)S(1)} %copy.7.hid, bf16[16,2,64,512]{3,2,1,0:T(8,128)(2,1)S(1)} %bitcast.4, s32[1,128]{1,0:T(1,128)S(1)} %bitcast.5, s32[1,512]{1,0:T(1,128)S(1)} %copy-done.1), custom_call_target="tpu_custom_call" | custom-call | flops 3221225472 | bytes 4194304 | tf_op jit(solution)/shard_map/pallas_call | solution.py:375
  107.8 1.3 %copy.11 = bf16[2048,512]{1,0:T(8,128)(2,1)} copy(bf16[2048,512]{1,0:T(8,128)(2,1)S(1)} %bitcast.3) | data formatting | bytes 4194304
  109.1 0.6 copy.12
Async XLA Ops:
  1.5 1.6 %copy-start = (bf16[2048,512]{1,0:T(8,128)(2,1)S(1)}, bf16[2048,512]{1,0:T(8,128)(2,1)}, u32[]{:S(2)}) copy-start(bf16[2048,512]{1,0:T(8,128)(2,1)} %param.5) | copy-start | bytes 6291460
  3.1 0.7 copy-start.1
  3.7 0.7 copy-start.2

commit v2 on v1

--- a/solution.py
+++ b/solution.py
@@ -23,13 +23,13 @@
 
 
 def kernel(
-    hid, w_hbm, lab, cnt,
+    hid_hbm, w_hbm, lab_hbm, cnt_hbm,
     gw_hbm, gh_out, loss_out,
-    wv, wt, zbuf, ht, part, bufa, bufb, rfl, rfr, cbuf, fcol, ebuf, stz, sty, gt,
+    wv, wt, zbuf, ht, part, bufa, bufb, rfl, rfr, cbuf, lbuf, fcol, eb, stz, sty, coef, gall,
     psend, pown, crecv, q, ya, yb, sa, sb, yl, yr, rz, zrb, gwv,
-    w_sem, gw_sem,
-    az_s, az_r, ax_s, ax_r, ct_s, ct_r, ay_s, ay_r, ac_s, ac_r,
-    b_s, b_r, sz_s, sz_r, sy_s, sy_r, d_s, d_r,
+    w_sem, in_sem, gw_sem,
+    az_s, az_r, ax_s, ax_r, ct_s, ct_r, lb_s, lb_r, ay_s, ay_r, ac_s, ac_r,
+    b_s, b_r, sz_s, sz_r, sy_s, sy_r, eb_s, eb_r, co_s, co_r,
     fc_s, fc_r, fy_s, fy_r, fz_s, fz_r,
 ):
     x = lax.axis_index("dp")
@@ -78,13 +78,13 @@
         rcopy(dst, dst, rs, rs, sibling).wait_recv()
 
     w_copy = pltpu.make_async_copy(w_hbm, wv, w_sem)
-    w_copy.start()
-
-    eye = (lax.broadcasted_iota(jnp.int32, (FEAT, FEAT), 0) == lax.broadcasted_iota(jnp.int32, (FEAT, FEAT), 1))
-    zbuf[z] = lax.dot_general(
-        eye.astype(F32).astype(BF), hid[...], (((1,), (1,)), ((), ())), preferred_element_type=F32
-    ).astype(BF)
-    cbuf[x] = cnt[...]
+    ins = [
+        pltpu.make_async_copy(hid_hbm, zbuf.at[z], in_sem.at[0]),
+        pltpu.make_async_copy(cnt_hbm, cbuf.at[x], in_sem.at[1]),
+        pltpu.make_async_copy(lab_hbm, lbuf.at[x], in_sem.at[2]),
+    ]
+    for copy in ins:
+        copy.start()
 
     barrier = pltpu.get_barrier_semaphore()
 
@@ -97,6 +97,9 @@
         pl.semaphore_signal(barrier, inc=1, device_id=to_q(k), device_id_type=MESH)
     for k in range(1, NX):
         pl.semaphore_signal(barrier, inc=1, device_id=to_x(k), device_id_type=MESH)
+    w_copy.start()
+    for copy in ins:
+        copy.wait()
     pl.semaphore_wait(barrier, 25)
 
     def start_z(i, _):
@@ -107,6 +110,7 @@
     lax.fori_loop(0, NZ - 1, start_z, 0)
     for k in range(1, NX):
         send(cbuf.at[x], cbuf.at[x], ct_s.at[k], ct_r.at[k], to_x(k))
+        send(lbuf.at[x], lbuf.at[x], lb_s.at[k], lb_r.at[k], to_x(k))
 
     w_copy.wait()
 
@@ -118,12 +122,14 @@
     lax.fori_loop(0, 8, turn, 0)
     for k in range(1, NX):
         recv(cbuf.at[xat(-k)], ct_r.at[k])
+        recv(lbuf.at[xat(-k)], lb_r.at[k])
     totals = cbuf[0] + cbuf[1] + cbuf[2] + cbuf[3]
     factor = lax.rsqrt(1.0 + totals.astype(F32))
     fcol[...] = jnp.broadcast_to(factor, (BATCH, VL)).T
 
     def wait_z(k, _):
         recv(zbuf.at[zat(-k)], az_r.at[k])
+        rcopy(zbuf.at[z], zbuf.at[z], az_s.at[k], az_r.at[k], sibling).wait_send()
         return 0
 
     lax.fori_loop(1, NZ, wait_z, 0)
@@ -170,21 +176,28 @@
             send(part.at[r, low], bufb, b_s.at[1], b_r.at[1], to_x(-1))
         if k == 3:
             send(part.at[r, low], rfl.at[low], b_s.at[2], b_r.at[2], to_x(1))
+        if k == 1:
+            send(part.at[r, top], rfr.at[top], b_s.at[4], b_r.at[4], to_x(-1))
+
+    def logits_relay(k):
+        r = xat(-k)
+        top, low = pl.ds(0, 256), pl.ds(256, 256)
+        if k == 3:
             recv(bufa, b_r.at[0])
             part[r, top] = part[r, top] + bufa[...]
             send(part.at[r, top], rfl.at[top], b_s.at[3], b_r.at[3], to_x(1))
         if k == 1:
-            send(part.at[r, top], rfr.at[top], b_s.at[4], b_r.at[4], to_x(-1))
             recv(bufb, b_r.at[1])
             part[r, low] = part[r, low] + bufb[...]
             send(part.at[r, low], rfr.at[low], b_s.at[5], b_r.at[5], to_x(-1))
 
-    stages = (hid_y, hid_relay, hid_core, logits_of)
-    order = (2, 1, 3, 0)
-    for t in range(len(order) + len(stages) - 1):
-        for j, stage in enumerate(stages):
-            if 0 <= t - j < len(order):
-                stage(order[t - j])
+    for stage, k in (
+        (hid_y, 0), (hid_y, 2), (hid_y, 1), (hid_y, 3),
+        (hid_relay, 0), (hid_relay, 2), (hid_relay, 1), (hid_relay, 3),
+        (hid_core, 2), (hid_core, 1), (logits_of, 2), (hid_core, 3), (logits_of, 1),
+        (hid_core, 0), (logits_of, 3), (logits_of, 0), (logits_relay, 3), (logits_relay, 1),
+    ):
+        stage(k)
 
     top, low = pl.ds(0, 256), pl.ds(256, 256)
     recv(rfl.at[low], b_r.at[2])
@@ -194,10 +207,12 @@
 
     logits = part[x] + rfl[...] + rfr[...]
     ids = lax.broadcasted_iota(jnp.int32, (VL, BATCH), 0) + (s * NY + y) * VL
-    hit = ids == lab[...]
+    hit = ids == lbuf[x]
     m0 = jnp.max(logits, axis=0, keepdims=True)
     e0 = jnp.exp(logits - m0)
-    ebuf[...] = e0
+    eb[x] = e0.astype(BF)
+    for k in (2, 1, 3):
+        send(eb.at[x], eb.at[x], eb_s.at[k], eb_r.at[k], to_x(k))
     zero = jnp.zeros((4, BATCH), F32)
     stz[z] = jnp.concatenate(
         [
@@ -224,6 +239,7 @@
 
     def wait_sz(k, _):
         recv(stz.at[zat(-k)], sz_r.at[k])
+        rcopy(stz.at[z], stz.at[z], sz_s.at[k], sz_r.at[k], sibling).wait_send()
         return 0
 
     lax.fori_loop(0, NZ - 1, start_sz, 0)
@@ -237,28 +253,29 @@
     m, total, target, weight = combine(sty)
     scaled = weight / jnp.mean(weight)
     loss_out[0] = jnp.sum(scaled * (jnp.log(total) + m - target)) / BATCH
-    rate = jnp.exp(m0 - m) / total
-    gt[x] = (scaled * (ebuf[...] * rate - hit.astype(F32))).astype(BF)
-
-    for d, e in ((0, 1), (1, -1)):
-        send(gt.at[x], gt.at[x], d_s.at[d], d_r.at[d], to_x(e))
-    for d, e in ((0, 1), (1, -1)):
-        recv(gt.at[xat(-e)], d_r.at[d])
-        ref = gt.at[xat(-e), pl.ds(256 * d, 256)]
-        send(ref, ref, d_s.at[2 + d], d_r.at[2 + d], to_x(e))
-    for d in (0, 1):
-        recv(gt.at[xat(2), pl.ds(256 * d, 256)], d_r.at[2 + d])
-
-    def gall():
-        return jnp.concatenate([gt[r] for r in range(NX)], axis=1)
-
+    coef[x] = jnp.concatenate([scaled * jnp.exp(m0 - m) / total, scaled, jnp.zeros((6, BATCH), F32)], axis=0)
+
+    for k in (2, 1, 3):
+        send(coef.at[x], coef.at[x], co_s.at[k], co_r.at[k], to_x(k))
+    for k in (0, 1, 3, 2):
+        r = xat(-k)
+        if k:
+            recv(eb.at[r], eb_r.at[k])
+            recv(coef.at[r], co_r.at[k])
+        v = coef[r]
+        gall[:, pl.ds(pl.multiple_of(r * BATCH, BATCH), BATCH)] = (
+            eb[r].astype(F32) * v[0:1] - jnp.where(ids == lbuf[r], v[1:2], 0.0)
+        ).astype(BF)
     def gh_dot(k):
         zz = lax.rem(zs + k, NX)
         rows = wv[pl.ds(ZL * zz, ZL), oc].reshape(256, VL)
-        psend[zz] = jnp.dot(rows, gall(), preferred_element_type=F32).astype(BF).reshape(ZL, NY, 16, 512)
+        psend[zz] = jnp.dot(rows, gall[...], preferred_element_type=F32).astype(BF).reshape(ZL, NY, 16, 512)
         send(psend.at[zz], crecv.at[zz], fc_s.at[k], fc_r.at[k], sibling)
+
+    def gh_own(k):
+        zz = lax.rem(zs + k, NX)
         rows = wv[pl.ds(ZL * zz, ZL), c].reshape(256, VL)
-        pown[zz] = jnp.dot(rows, gall(), preferred_element_type=F32).reshape(ZL, NY, 16, 512)
+        pown[zz] = jnp.dot(rows, gall[...], preferred_element_type=F32).reshape(ZL, NY, 16, 512)
 
     def gh_core(k):
         zz = lax.rem(zs + k, NX)
@@ -292,16 +309,14 @@
             l = lax.rem(zl0 + j, ZL)
             send(rz.at[zz, l], zrb.at[z], fz_s.at[k, j], fz_r.at[z], to_z(ZL * zz + l))
 
-    stages = (gh_dot, gh_core, gh_relay, gh_z)
-    order = (2, 1, 3, 0)
-    for t in range(len(order) + len(stages) - 1):
-        for j, stage in enumerate(stages):
-            if 0 <= t - j < len(order):
-                stage(order[t - j])
+    for stages in ((gh_dot,), (gh_own, gh_core), (gh_relay,), (gh_z,)):
+        for k in (2, 1, 3, 0):
+            for stage in stages:
+                stage(k)
 
     def gw_tile(i, _):
         lhs = jnp.concatenate([ht[r, i // 2, lax.rem(i, 2)].reshape(256, BATCH) for r in range(NX)], axis=1)
-        gwv[i] = lax.dot_general(lhs, gall(), (((1,), (1,)), ((), ())), preferred_element_type=F32).astype(BF)
+        gwv[i] = lax.dot_general(lhs, gall[...], (((1,), (1,)), ((), ())), preferred_element_type=F32).astype(BF)
         pltpu.make_async_copy(gwv.at[i], gw_hbm.at[i], gw_sem.at[i]).start()
         return 0
 
@@ -322,12 +337,6 @@
 
     lax.fori_loop(0, 8, gw_wait, 0)
 
-    def done_z(k, _):
-        rcopy(zbuf.at[z], zbuf.at[z], az_s.at[k], az_r.at[k], sibling).wait_send()
-        rcopy(stz.at[z], stz.at[z], sz_s.at[k], sz_r.at[k], sibling).wait_send()
-        return 0
-
-    lax.fori_loop(1, NZ, done_z, 0)
     for d in sends:
         d.wait_send()
 
@@ -346,11 +355,13 @@
         v((VL, BATCH), F32),
         v((VL, BATCH), F32),
         v((NX, 1, VL), jnp.int32),
+        v((NX, 1, BATCH), jnp.int32),
         v((VL, BATCH), F32),
-        v((VL, BATCH), F32),
+        v((NX, VL, BATCH), BF),
         v((NZ, 8, BATCH), F32),
         v((8, 8, BATCH), F32),
-        v((NX, VL, BATCH), BF),
+        v((NX, 8, BATCH), F32),
+        v((VL, NX * BATCH), BF),
         v((NX, ZL, NY, 16, 512), BF),
         v((NX, ZL, NY, 16, 512), F32),
         v((NX, ZL, NY, 16, 512), BF),
@@ -364,14 +375,14 @@
         v((NX, ZL, 16, 512), BF),
         v((NZ, 16, 512), BF),
         v((8, 256, VL), BF),
-        dma, dma((8,)),
-        dma((16,)), dma((16,)), dma((4,)), dma((4,)), dma((4,)), dma((4,)),
+        dma, dma((3,)), dma((8,)),
+        dma((16,)), dma((16,)), dma((4,)), dma((4,)), dma((4,)), dma((4,)), dma((4,)), dma((4,)),
         dma((4, 4)), dma((4, 4)), dma((4,)), dma((4,)),
-        dma((6,)), dma((6,)), dma((16,)), dma((16,)), dma((8,)), dma((8,)), dma((4,)), dma((4,)),
+        dma((6,)), dma((6,)), dma((16,)), dma((16,)), dma((8,)), dma((8,)), dma((4,)), dma((4,)), dma((4,)), dma((4,)),
         dma((4,)), dma((4,)), dma((4, 6)), dma((4, 6)), dma((4, 4)), dma((16,)),
     ]
     vmem = pl.BlockSpec(memory_space=pltpu.VMEM)
-    hbm = pl.BlockSpec(memory_space=pl.ANY)
+    hbm = pl.BlockSpec(memory_space=pltpu.HBM)
     gw, gh, loss = pl.pallas_call(
         kernel,
         out_shape=(
@@ -379,14 +390,14 @@
             jax.ShapeDtypeStruct((16, 512), BF),
             jax.ShapeDtypeStruct((1,), F32),
         ),
-        in_specs=[vmem, hbm, vmem, vmem],
-        out_specs=(hbm, vmem, pl.BlockSpec(memory_space=pltpu.SMEM)),
+        in_specs=[hbm] * 4,
+        out_specs=(pl.BlockSpec(memory_space=pl.ANY), vmem, pl.BlockSpec(memory_space=pltpu.SMEM)),
         scratch_shapes=scratch,
         compiler_params=pltpu.CompilerParams(
-            collective_id=0, has_side_effects=True, vmem_limit_bytes=48 * 1024 * 1024
+            collective_id=0, has_side_effects=True, vmem_limit_bytes=63 * 1024 * 1024
         ),
         cost_estimate=pl.CostEstimate(flops=3 * 2**30, bytes_accessed=2**22, transcendentals=2**16),
-    )(hidden, weight.reshape(16, 2, 64, VL), labels.reshape(1, BATCH), counts)
+    )(hidden.T, weight.reshape(16, 2, 64, VL), labels.reshape(1, BATCH), counts)
     return gw.reshape(2048, VL), gh, loss
 
 

time: 112 us -> 104 us (0.929)
  Pallas kernels: 103 us -> 97.6 us
  local copies, waits for them, and re-layouts: 5.68 us -> 3.66 us
    pallas_call x1, Pallas kernels: 103 us -> 97.6 us  [body(): pl.pallas_call(kernel, out_shape=(jax.ShapeDtypeStruct((8, 256, VL), BF),...]
    unnamed x9 -> x4, local copies, waits for them, and re-layouts: 5.68 us -> 3.66 us
where the time goes in v2:
time: 104 us
  Pallas kernels  97.6 us (94%)
  local copies, waits for them, and re-layouts  3.66 us (4%)
  between operations  2.32 us (2%)
    pallas_call x1, Pallas kernels, body(): pl.pallas_call(kernel, out_shape=(jax.ShapeDtypeStruct((8, 256, VL), BF),...  97.6 us
    unnamed x4, local copies, waits for them, and re-layouts  3.66 us

profile of v2, /device:TPU:1, one launch (start us, length us, event | category | flops | bytes accessed | tf_op | source)
XLA Modules:
  0.0 103.6 jit_solution(4822383682113400633)
XLA Ops:
  0.6 97.6 %shard_map.67 = (bf16[8,256,512]{2,1,0:T(8,128)(2,1)}, bf16[16,512]{1,0:T(8,128)(2,1)}, f32[1]{0:T(128)}) custom-call(bf16[64,128]{1,0:T(8,128)(2,1)} %bitcast.6, bf16[16,2,64,512]{3,2,1,0:T(8,128)(2,1)} %bitcast.5, s32[1,128]{1,0:T(1,128)} %bitcast.7, s32[1,512]{1,0:T(1,128)} %cnt_hbm.1), custom_call_target="tpu_custom_call" | custom-call | flops 3221225472 | bytes 4194304 | tf_op jit(solution)/shard_map/pallas_call | solution.py:386
  98.3 0.0 copy-start
  98.3 3.0 %copy.10 = bf16[2048,512]{1,0:T(8,128)(2,1)} copy(bf16[2048,512]{1,0:T(8,128)(2,1)} %bitcast.4) | data formatting | bytes 4194304
  101.3 0.0 copy-done
  101.3 0.6 copy.11
Async XLA Ops:
  98.3 3.1 %copy-start = (bf16[16,512]{1,0:T(8,128)(2,1)S(1)}, bf16[16,512]{1,0:T(8,128)(2,1)}, u32[]{:S(2)}) copy-start(bf16[16,512]{1,0:T(8,128)(2,1)} %get-tuple-element.13) | copy-start | bytes 49156

commit v3 on v2

--- a/solution.py
+++ b/solution.py
@@ -17,6 +17,18 @@
 F32 = jnp.float32
 
 
+GATHER = (
+    ("yd", 0), ("yd", 2), ("yd", 1), ("yd", 3), ("cored", 2), ("cored", 1),
+    ("logits", 2), ("cored", 3), ("logits", 1), ("cored", 0), ("logits", 3), ("logits", 0),
+    ("sum", 3), ("sum", 1),
+)
+REDUCE = (
+    ("dot", 2), ("dot", 1), ("dot", 3), ("dot", 0), ("own", 2), ("yd", 2), ("own", 1), ("y", 1), ("own", 3), ("y", 3),
+    ("own", 0), ("y", 0), ("gw", 0), ("gw", 1), ("relay", 1), ("zd", 2), ("relay", 3), ("z", 1), ("relay", 0), ("gw", 2), ("z", 3),
+    ("gw", 3), ("z", 0), ("gw", 4), ("gw", 5), ("gw", 6), ("gw", 7),
+)
+
+
 def spread(i):
     half = (i + 1) // 2
     return NZ // 2 + (1 - 2 * lax.rem(i, 2)) * half
@@ -26,7 +38,7 @@
     hid_hbm, w_hbm, lab_hbm, cnt_hbm,
     gw_hbm, gh_out, loss_out,
     wv, wt, zbuf, ht, part, bufa, bufb, rfl, rfr, cbuf, lbuf, fcol, eb, stz, sty, coef, gall,
-    psend, pown, crecv, q, ya, yb, sa, sb, yl, yr, rz, zrb, gwv,
+    psend, pown, crecv, q, ya, yb, sa, sb, yl, yr, y2, rz, zrb, gwv,
     w_sem, in_sem, gw_sem,
     az_s, az_r, ax_s, ax_r, ct_s, ct_r, lb_s, lb_r, ay_s, ay_r, ac_s, ac_r,
     b_s, b_r, sz_s, sz_r, sy_s, sy_r, eb_s, eb_r, co_s, co_r,
@@ -88,11 +100,11 @@
 
     barrier = pltpu.get_barrier_semaphore()
 
-    def greet_z(k, _):
-        pl.semaphore_signal(barrier, inc=1, device_id=to_z(zat(k)), device_id_type=MESH)
-        return 0
-
-    lax.fori_loop(1, NZ, greet_z, 0)
+    def greet_z(i, _):
+        pl.semaphore_signal(barrier, inc=1, device_id=to_z(zat(spread(i))), device_id_type=MESH)
+        return 0
+
+    lax.fori_loop(0, NZ - 1, greet_z, 0)
     for k in range(1, 8):
         pl.semaphore_signal(barrier, inc=1, device_id=to_q(k), device_id_type=MESH)
     for k in range(1, NX):
@@ -145,6 +157,19 @@
             recv(ht.at[r, :, c, y], ax_r.at[k])
         for d, e in ((0, 1), (1, -1)):
             send(ht.at[r, :, c, y], ht.at[r, :, c, y], ay_s.at[k, d], ay_r.at[k, d], to_y(e))
+
+    def hid_yd(k):
+        r = xat(-k)
+        if k:
+            recv(ht.at[r, :, c, y], ax_r.at[k])
+        for d, e in ((2, 2), (0, 1), (1, -1)):
+            send(ht.at[r, :, c, y], ht.at[r, :, c, y], ay_s.at[k, d], ay_r.at[k, d], to_y(e))
+
+    def hid_cored(k):
+        r = xat(-k)
+        for d, e in ((0, 1), (1, -1), (2, 2)):
+            recv(ht.at[r, :, c, yat(-e)], ay_r.at[k, d])
+        send(ht.at[r, :, c], ht.at[r, :, c], ac_s.at[k], ac_r.at[k], sibling)
 
     def hid_relay(k):
         r = xat(-k)
@@ -191,13 +216,12 @@
             part[r, low] = part[r, low] + bufb[...]
             send(part.at[r, low], rfr.at[low], b_s.at[5], b_r.at[5], to_x(-1))
 
-    for stage, k in (
-        (hid_y, 0), (hid_y, 2), (hid_y, 1), (hid_y, 3),
-        (hid_relay, 0), (hid_relay, 2), (hid_relay, 1), (hid_relay, 3),
-        (hid_core, 2), (hid_core, 1), (logits_of, 2), (hid_core, 3), (logits_of, 1),
-        (hid_core, 0), (logits_of, 3), (logits_of, 0), (logits_relay, 3), (logits_relay, 1),
-    ):
-        stage(k)
+    run = {
+        "y": hid_y, "yd": hid_yd, "relay": hid_relay, "core": hid_core, "cored": hid_cored,
+        "logits": logits_of, "sum": logits_relay,
+    }
+    for name, k in GATHER:
+        run[name](k)
 
     top, low = pl.ds(0, 256), pl.ds(256, 256)
     recv(rfl.at[low], b_r.at[2])
@@ -276,11 +300,17 @@
         zz = lax.rem(zs + k, NX)
         rows = wv[pl.ds(ZL * zz, ZL), c].reshape(256, VL)
         pown[zz] = jnp.dot(rows, gall[...], preferred_element_type=F32).reshape(ZL, NY, 16, 512)
-
-    def gh_core(k):
-        zz = lax.rem(zs + k, NX)
         recv(crecv.at[zz], fc_r.at[k])
         q[zz] = (pown[zz] + crecv[zz].astype(F32)).astype(BF)
+
+    def gh_yd(k):
+        zz = lax.rem(zs + k, NX)
+        send(q.at[zz, :, yat(2)], y2.at[k], fy_s.at[k, 2], fy_r.at[k, 2], to_y(2))
+        send(q.at[zz, :, yat(1)], yl.at[k], fy_s.at[k, 0], fy_r.at[k, 0], to_y(1))
+        send(q.at[zz, :, yat(-1)], yr.at[k], fy_s.at[k, 1], fy_r.at[k, 1], to_y(-1))
+
+    def gh_y(k):
+        zz = lax.rem(zs + k, NX)
         up, down = pl.ds(0, 2), pl.ds(2, 2)
         send(q.at[zz, up, yat(2)], ya.at[k], fy_s.at[k, 0], fy_r.at[k, 0], to_y(1))
         send(q.at[zz, down, yat(2)], yb.at[k], fy_s.at[k, 1], fy_r.at[k, 1], to_y(-1))
@@ -305,22 +335,32 @@
         recv(yl.at[k, up], fy_r.at[k, 4])
         recv(yr.at[k, down], fy_r.at[k, 5])
         rz[zz] = (q[zz, :, y].astype(F32) + yl[k].astype(F32) + yr[k].astype(F32)).astype(BF)
+        gh_send(k)
+
+    def gh_zd(k):
+        zz = lax.rem(zs + k, NX)
+        for ref, d in ((yl, 0), (yr, 1), (y2, 2)):
+            recv(ref.at[k], fy_r.at[k, d])
+        near = yl[k].astype(F32) + yr[k].astype(F32)
+        rz[zz] = (q[zz, :, y].astype(F32) + near + y2[k].astype(F32)).astype(BF)
+        gh_send(k)
+
+    def gh_send(k):
+        zz = lax.rem(zs + k, NX)
         for j in range(0 if k else 1, ZL):
             l = lax.rem(zl0 + j, ZL)
             send(rz.at[zz, l], zrb.at[z], fz_s.at[k, j], fz_r.at[z], to_z(ZL * zz + l))
 
-    for stages in ((gh_dot,), (gh_own, gh_core), (gh_relay,), (gh_z,)):
-        for k in (2, 1, 3, 0):
-            for stage in stages:
-                stage(k)
-
-    def gw_tile(i, _):
-        lhs = jnp.concatenate([ht[r, i // 2, lax.rem(i, 2)].reshape(256, BATCH) for r in range(NX)], axis=1)
+    def gw_tile(i):
+        lhs = jnp.concatenate([ht[r, i // 2, i % 2].reshape(256, BATCH) for r in range(NX)], axis=1)
         gwv[i] = lax.dot_general(lhs, gall[...], (((1,), (1,)), ((), ())), preferred_element_type=F32).astype(BF)
         pltpu.make_async_copy(gwv.at[i], gw_hbm.at[i], gw_sem.at[i]).start()
-        return 0
-
-    lax.fori_loop(0, 8, gw_tile, 0)
+
+    run = {
+        "dot": gh_dot, "own": gh_own, "y": gh_y, "yd": gh_yd, "relay": gh_relay, "z": gh_z, "zd": gh_zd, "gw": gw_tile,
+    }
+    for name, k in REDUCE:
+        run[name](k)
 
     zrb[z] = rz[zs, zl0]
 
@@ -339,6 +379,25 @@
 
     for d in sends:
         d.wait_send()
+
+
+def hand_over(*refs):
+    ins, outs, bufs, (in_sem, out_sem) = refs[:3], refs[3:6], refs[6:9], refs[9:]
+    pieces = [(0, i) for i in range(8)] + [(1, None), (2, None)]
+
+    def copy(src, dst, piece, sem):
+        j, i = piece
+        n = pieces.index(piece)
+        a, b = (src[j], dst[j]) if i is None else (src[j].at[i], dst[j].at[i])
+        return pltpu.make_async_copy(a, b, sem.at[n])
+
+    for piece in pieces:
+        copy(ins, bufs, piece, in_sem).start()
+    for piece in pieces:
+        copy(ins, bufs, piece, in_sem).wait()
+        copy(bufs, outs, piece, out_sem).start()
+    for piece in pieces:
+        copy(bufs, outs, piece, out_sem).wait()
 
 
 def body(hidden, weight, labels, counts):
@@ -373,6 +432,7 @@
         v((NX, ZL, 16, 512), BF),
         v((NX, ZL, 16, 512), BF),
         v((NX, ZL, 16, 512), BF),
+        v((NX, ZL, 16, 512), BF),
         v((NZ, 16, 512), BF),
         v((8, 256, VL), BF),
         dma, dma((3,)), dma((8,)),
@@ -383,21 +443,32 @@
     ]
     vmem = pl.BlockSpec(memory_space=pltpu.VMEM)
     hbm = pl.BlockSpec(memory_space=pltpu.HBM)
-    gw, gh, loss = pl.pallas_call(
+    shapes = (
+        jax.ShapeDtypeStruct((8, 256, VL), BF),
+        jax.ShapeDtypeStruct((16, 512), BF),
+        jax.ShapeDtypeStruct((1,), F32),
+    )
+    smem = pl.BlockSpec(memory_space=pltpu.SMEM)
+    made = pl.pallas_call(
         kernel,
-        out_shape=(
-            jax.ShapeDtypeStruct((8, 256, VL), BF),
-            jax.ShapeDtypeStruct((16, 512), BF),
-            jax.ShapeDtypeStruct((1,), F32),
-        ),
+        out_shape=shapes,
         in_specs=[hbm] * 4,
-        out_specs=(pl.BlockSpec(memory_space=pl.ANY), vmem, pl.BlockSpec(memory_space=pltpu.SMEM)),
+        out_specs=(pl.BlockSpec(memory_space=pl.ANY), vmem, smem),
         scratch_shapes=scratch,
         compiler_params=pltpu.CompilerParams(
             collective_id=0, has_side_effects=True, vmem_limit_bytes=63 * 1024 * 1024
         ),
         cost_estimate=pl.CostEstimate(flops=3 * 2**30, bytes_accessed=2**22, transcendentals=2**16),
     )(hidden.T, weight.reshape(16, 2, 64, VL), labels.reshape(1, BATCH), counts)
+    gw, gh, loss = pl.pallas_call(
+        hand_over,
+        out_shape=shapes,
+        in_specs=[hbm] * 3,
+        out_specs=(hbm,) * 3,
+        scratch_shapes=[
+            v((8, 256, VL), BF), v((16, 512), BF), pltpu.SMEM((1,), F32), dma((10,)), dma((10,)),
+        ],
+    )(*made)
     return gw.reshape(2048, VL), gh, loss
 
 

time: 104 us -> 97.7 us (0.939)
  local copies, waits for them, and re-layouts: 3.66 us -> 0 us
  between operations: 2.32 us -> 0.64 us
    unnamed x4 -> x0, local copies, waits for them, and re-layouts: 3.66 us -> none
    pallas_call x1 -> x2, Pallas kernels: 97.6 us -> 96.9 us  [the longest x1 93.9 us: body(): pl.pallas_call(kernel, out_shape=shapes, in_specs=[hbm] * 4, out_specs=(p...]
where the time goes in v3:
time: 97.7 us; the launch traced here: 97.5 us
  Pallas kernels  96.9 us (99%)
    pallas_call x1, Pallas kernels, body(): pl.pallas_call(kernel, out_shape=shapes, in_specs=[hbm] * 4, out_specs=(p...  93.9 us
    pallas_call x1, Pallas kernels, body(): pl.pallas_call(hand_over, out_shape=shapes, in_specs=[hbm] * 3, out_specs...  2.98 us

profile of v3, /device:TPU:1, one launch (start us, length us, event | category | flops | bytes accessed | tf_op | source)
XLA Modules:
  0.0 97.5 jit_solution(10481010724707238703)
XLA Ops:
  0.6 93.9 %shard_map.67 = (bf16[8,256,512]{2,1,0:T(8,128)(2,1)}, bf16[16,512]{1,0:T(8,128)(2,1)}, f32[1]{0:T(128)}) custom-call(bf16[64,128]{1,0:T(8,128)(2,1)} %bitcast.6, bf16[16,2,64,512]{3,2,1,0:T(8,128)(2,1)} %bitcast.4, s32[1,128]{1,0:T(1,128)} %bitcast.7, s32[1,512]{1,0:T(1,128)} %cnt_hbm.1), custom_call_target="tpu_custom_call" | custom-call | flops 3221225472 | bytes 4194304 | tf_op jit(solution)/shard_map/pallas_call | solution.py:452
  94.6 3.0 %shard_map.68 = (bf16[8,256,512]{2,1,0:T(8,128)(2,1)}, bf16[16,512]{1,0:T(8,128)(2,1)}, f32[1]{0:T(128)}) custom-call(bf16[8,256,512]{2,1,0:T(8,128)(2,1)} %get-tuple-element.9.refs_0_, bf16[16,512]{1,0:T(8,128)(2,1)} %get-tuple-element.10.refs_1_, f32[1]{0:T(128)} %get-tuple-element.11.refs_2_), custom_call_target="tpu_custom_call" | custom-call | tf_op jit(solution)/shard_map/pallas_call | solution.py:463

commit v4 on v2

--- a/solution.py
+++ b/solution.py
@@ -17,6 +17,19 @@
 F32 = jnp.float32
 
 
+GATHER = (
+    ("x", 0, 0),
+    ("y", 2, 0), ("y", 1, 0), ("y", 3, 0),  ("x", 0, 1), ("y", 2, 1), ("y", 1, 1), ("y", 3, 1),
+    ("core", 2), ("core", 1), ("logits", 2), ("core", 3), ("logits", 1), ("core", 0), ("logits", 3), ("logits", 0),
+    ("sum", 3), ("sum", 1),
+)
+REDUCE = (
+    ("dot", 2), ("dot", 1), ("dot", 3), ("dot", 0), ("own", 2), ("yd", 2, 0), ("yd", 2, 1), ("own", 1), ("yd", 1, 0), ("yd", 1, 1),
+    ("own", 3), ("yd", 3, 0), ("yd", 3, 1), ("own", 0), ("y", 0), ("gw", 0), ("gw", 1), ("zd", 2, 0), ("zd", 2, 1), ("relay", 0),
+    ("zd", 1, 0), ("zd", 1, 1), ("zd", 3, 0), ("zd", 3, 1), ("gw", 2), ("gw", 3), ("z", 0), ("gw", 4), ("gw", 5), ("gw", 6), ("gw", 7),
+)
+
+
 def spread(i):
     half = (i + 1) // 2
     return NZ // 2 + (1 - 2 * lax.rem(i, 2)) * half
@@ -24,10 +37,10 @@
 
 def kernel(
     hid_hbm, w_hbm, lab_hbm, cnt_hbm,
-    gw_hbm, gh_out, loss_out,
+    gwv, gh_out, loss_out,
     wv, wt, zbuf, ht, part, bufa, bufb, rfl, rfr, cbuf, lbuf, fcol, eb, stz, sty, coef, gall,
-    psend, pown, crecv, q, ya, yb, sa, sb, yl, yr, rz, zrb, gwv,
-    w_sem, in_sem, gw_sem,
+    psend, pown, crecv, q, ya, yb, sa, sb, yl, yr, y2, rz, zrb,
+    w_sem, in_sem,
     az_s, az_r, ax_s, ax_r, ct_s, ct_r, lb_s, lb_r, ay_s, ay_r, ac_s, ac_r,
     b_s, b_r, sz_s, sz_r, sy_s, sy_r, eb_s, eb_r, co_s, co_r,
     fc_s, fc_r, fy_s, fy_r, fz_s, fz_r,
@@ -74,6 +87,10 @@
         d.start()
         sends.append(d)
 
+    def play(run, schedule):
+        for name, *at in schedule:
+            run[name](*at)
+
     def recv(dst, rs):
         rcopy(dst, dst, rs, rs, sibling).wait_recv()
 
@@ -88,11 +105,11 @@
 
     barrier = pltpu.get_barrier_semaphore()
 
-    def greet_z(k, _):
-        pl.semaphore_signal(barrier, inc=1, device_id=to_z(zat(k)), device_id_type=MESH)
+    def greet_z(i, _):
+        pl.semaphore_signal(barrier, inc=1, device_id=to_z(zat(spread(i))), device_id_type=MESH)
         return 0
 
-    lax.fori_loop(1, NZ, greet_z, 0)
+    lax.fori_loop(0, NZ - 1, greet_z, 0)
     for k in range(1, 8):
         pl.semaphore_signal(barrier, inc=1, device_id=to_q(k), device_id_type=MESH)
     for k in range(1, NX):
@@ -102,12 +119,19 @@
         copy.wait()
     pl.semaphore_wait(barrier, 25)
 
-    def start_z(i, _):
-        k = spread(i)
-        rcopy(zbuf.at[z], zbuf.at[z], az_s.at[k], az_r.at[k], to_z(zat(k))).start()
-        return 0
-
-    lax.fori_loop(0, NZ - 1, start_z, 0)
+    halves = [pl.ds(0, FEAT // 2), pl.ds(FEAT // 2, FEAT // 2)]
+
+    def start_z(h):
+        def start(i, _):
+            k = spread(i)
+            ref = zbuf.at[z, halves[h]]
+            rcopy(ref, ref, az_s.at[h, k], az_r.at[h, k], to_z(zat(k))).start()
+            return 0
+
+        lax.fori_loop(0, NZ - 1, start, 0)
+
+    start_z(0)
+    start_z(1)
     for k in range(1, NX):
         send(cbuf.at[x], cbuf.at[x], ct_s.at[k], ct_r.at[k], to_x(k))
         send(lbuf.at[x], lbuf.at[x], lb_s.at[k], lb_r.at[k], to_x(k))
@@ -127,37 +151,36 @@
     factor = lax.rsqrt(1.0 + totals.astype(F32))
     fcol[...] = jnp.broadcast_to(factor, (BATCH, VL)).T
 
-    def wait_z(k, _):
-        recv(zbuf.at[zat(-k)], az_r.at[k])
-        rcopy(zbuf.at[z], zbuf.at[z], az_s.at[k], az_r.at[k], sibling).wait_send()
-        return 0
-
-    lax.fori_loop(1, NZ, wait_z, 0)
-
-    for k in (2, 1, 3):
-        to = xat(k)
-        send(zbuf.at[pl.ds(ZL * to, ZL)], ht.at[x, :, c, y], ax_s.at[k], ax_r.at[k], to_x(k))
-    ht[x, :, c, y] = zbuf[pl.ds(ZL * x, ZL)]
-
-    def hid_y(k):
+    def hid_x(_, h):
+        def wait_z(k, _):
+            ref = zbuf.at[z, halves[h]]
+            recv(zbuf.at[zat(-k), halves[h]], az_r.at[h, k])
+            rcopy(ref, ref, az_s.at[h, k], az_r.at[h, k], sibling).wait_send()
+            return 0
+
+        lax.fori_loop(1, NZ, wait_z, 0)
+        for k in (2, 1, 3):
+            to = xat(k)
+            send(
+                zbuf.at[pl.ds(ZL * to, ZL), halves[h]], ht.at[x, :, c, y, halves[h]],
+                ax_s.at[h, k], ax_r.at[h, k], to_x(k),
+            )
+        ht[x, :, c, y, halves[h]] = zbuf[pl.ds(ZL * x, ZL), halves[h]]
+        hid_y(0, h)
+
+    def hid_y(k, h):
         r = xat(-k)
+        ref = ht.at[r, :, c, y, halves[h]]
         if k:
-            recv(ht.at[r, :, c, y], ax_r.at[k])
-        for d, e in ((0, 1), (1, -1)):
-            send(ht.at[r, :, c, y], ht.at[r, :, c, y], ay_s.at[k, d], ay_r.at[k, d], to_y(e))
-
-    def hid_relay(k):
-        r = xat(-k)
-        for d, e in ((0, 1), (1, -1)):
-            recv(ht.at[r, :, c, yat(-e)], ay_r.at[k, d])
-            half = pl.ds(2 * d, 2)
-            ref = ht.at[r, half, c, yat(-e)]
-            send(ref, ref, ay_s.at[k, 2 + d], ay_r.at[k, 2 + d], to_y(e))
+            recv(ref, ax_r.at[h, k])
+        for e in (2, 1, 3):
+            send(ref, ref, ay_s.at[h, k, e], ay_r.at[h, k, e], to_y(e))
 
     def hid_core(k):
         r = xat(-k)
-        for d in (0, 1):
-            recv(ht.at[r, pl.ds(2 * d, 2), c, yat(2)], ay_r.at[k, 2 + d])
+        for h in (0, 1):
+            for e in (1, 3, 2):
+                recv(ht.at[r, :, c, yat(-e), halves[h]], ay_r.at[h, k, e])
         send(ht.at[r, :, c], ht.at[r, :, c], ac_s.at[k], ac_r.at[k], sibling)
 
     def logits_of(k):
@@ -191,13 +214,8 @@
             part[r, low] = part[r, low] + bufb[...]
             send(part.at[r, low], rfr.at[low], b_s.at[5], b_r.at[5], to_x(-1))
 
-    for stage, k in (
-        (hid_y, 0), (hid_y, 2), (hid_y, 1), (hid_y, 3),
-        (hid_relay, 0), (hid_relay, 2), (hid_relay, 1), (hid_relay, 3),
-        (hid_core, 2), (hid_core, 1), (logits_of, 2), (hid_core, 3), (logits_of, 1),
-        (hid_core, 0), (logits_of, 3), (logits_of, 0), (logits_relay, 3), (logits_relay, 1),
-    ):
-        stage(k)
+    run = {"x": hid_x, "y": hid_y, "core": hid_core, "logits": logits_of, "sum": logits_relay}
+    play(run, GATHER)
 
     top, low = pl.ds(0, 256), pl.ds(256, 256)
     recv(rfl.at[low], b_r.at[2])
@@ -276,11 +294,18 @@
         zz = lax.rem(zs + k, NX)
         rows = wv[pl.ds(ZL * zz, ZL), c].reshape(256, VL)
         pown[zz] = jnp.dot(rows, gall[...], preferred_element_type=F32).reshape(ZL, NY, 16, 512)
-
-    def gh_core(k):
-        zz = lax.rem(zs + k, NX)
         recv(crecv.at[zz], fc_r.at[k])
         q[zz] = (pown[zz] + crecv[zz].astype(F32)).astype(BF)
+
+    def gh_yd(k, h):
+        zz = lax.rem(zs + k, NX)
+        two = pl.ds(2 * h, 2)
+        for e, ref in ((2, y2), (1, yl), (3, yr)):
+            n = 3 * h + e - 1
+            send(q.at[zz, two, yat(e)], ref.at[k, two], fy_s.at[k, n], fy_r.at[k, n], to_y(e))
+
+    def gh_y(k):
+        zz = lax.rem(zs + k, NX)
         up, down = pl.ds(0, 2), pl.ds(2, 2)
         send(q.at[zz, up, yat(2)], ya.at[k], fy_s.at[k, 0], fy_r.at[k, 0], to_y(1))
         send(q.at[zz, down, yat(2)], yb.at[k], fy_s.at[k, 1], fy_r.at[k, 1], to_y(-1))
@@ -309,18 +334,24 @@
             l = lax.rem(zl0 + j, ZL)
             send(rz.at[zz, l], zrb.at[z], fz_s.at[k, j], fz_r.at[z], to_z(ZL * zz + l))
 
-    for stages in ((gh_dot,), (gh_own, gh_core), (gh_relay,), (gh_z,)):
-        for k in (2, 1, 3, 0):
-            for stage in stages:
-                stage(k)
-
-    def gw_tile(i, _):
-        lhs = jnp.concatenate([ht[r, i // 2, lax.rem(i, 2)].reshape(256, BATCH) for r in range(NX)], axis=1)
+    def gh_zd(k, h):
+        zz = lax.rem(zs + k, NX)
+        two = pl.ds(2 * h, 2)
+        for e, ref in ((1, yl), (3, yr), (2, y2)):
+            recv(ref.at[k, two], fy_r.at[k, 3 * h + e - 1])
+        near = yl[k, two].astype(F32) + yr[k, two].astype(F32)
+        rz[zz, two] = (q[zz, two, y].astype(F32) + near + y2[k, two].astype(F32)).astype(BF)
+        for j in (2 * h, 2 * h + 1):
+            send(rz.at[zz, j], zrb.at[z], fz_s.at[k, j], fz_r.at[z], to_z(ZL * zz + j))
+
+    def gw_tile(i):
+        lhs = jnp.concatenate([ht[r, i // 2, i % 2].reshape(256, BATCH) for r in range(NX)], axis=1)
         gwv[i] = lax.dot_general(lhs, gall[...], (((1,), (1,)), ((), ())), preferred_element_type=F32).astype(BF)
-        pltpu.make_async_copy(gwv.at[i], gw_hbm.at[i], gw_sem.at[i]).start()
-        return 0
-
-    lax.fori_loop(0, 8, gw_tile, 0)
+
+    run = {
+        "dot": gh_dot, "own": gh_own, "y": gh_y, "yd": gh_yd, "relay": gh_relay, "z": gh_z, "zd": gh_zd, "gw": gw_tile,
+    }
+    play(run, REDUCE)
 
     zrb[z] = rz[zs, zl0]
 
@@ -331,14 +362,22 @@
     lax.fori_loop(1, NZ, wait_fz, 0)
     gh_out[...] = jnp.sum(zrb[...].astype(F32), axis=0).astype(BF)
 
-    def gw_wait(i, _):
-        pltpu.make_async_copy(gwv.at[i], gw_hbm.at[i], gw_sem.at[i]).wait()
-        return 0
-
-    lax.fori_loop(0, 8, gw_wait, 0)
-
     for d in sends:
         d.wait_send()
+
+
+def hand_over(gw_in, gh_in, loss_in, gw_out, gh_out, loss_out, held, sem):
+    copies = [pltpu.make_async_copy(gw_in.at[i], gw_out.at[i], sem.at[i]) for i in range(8)]
+    copies.append(pltpu.make_async_copy(gh_in, gh_out, sem.at[8]))
+    first = pltpu.make_async_copy(loss_in, held, sem.at[9])
+    first.start()
+    for copy in copies:
+        copy.start()
+    first.wait()
+    copies.append(pltpu.make_async_copy(held, loss_out, sem.at[9]))
+    copies[-1].start()
+    for copy in copies:
+        copy.wait()
 
 
 def body(hidden, weight, labels, counts):
@@ -373,31 +412,42 @@
         v((NX, ZL, 16, 512), BF),
         v((NX, ZL, 16, 512), BF),
         v((NX, ZL, 16, 512), BF),
+        v((NX, ZL, 16, 512), BF),
         v((NZ, 16, 512), BF),
-        v((8, 256, VL), BF),
-        dma, dma((3,)), dma((8,)),
-        dma((16,)), dma((16,)), dma((4,)), dma((4,)), dma((4,)), dma((4,)), dma((4,)), dma((4,)),
-        dma((4, 4)), dma((4, 4)), dma((4,)), dma((4,)),
+        dma, dma((3,)),
+        dma((2, 16)), dma((2, 16)), dma((2, 4)), dma((2, 4)), dma((4,)), dma((4,)), dma((4,)), dma((4,)),
+        dma((2, 4, 4)), dma((2, 4, 4)), dma((4,)), dma((4,)),
         dma((6,)), dma((6,)), dma((16,)), dma((16,)), dma((8,)), dma((8,)), dma((4,)), dma((4,)), dma((4,)), dma((4,)),
         dma((4,)), dma((4,)), dma((4, 6)), dma((4, 6)), dma((4, 4)), dma((16,)),
     ]
     vmem = pl.BlockSpec(memory_space=pltpu.VMEM)
     hbm = pl.BlockSpec(memory_space=pltpu.HBM)
-    gw, gh, loss = pl.pallas_call(
+    args = (hidden.T, weight.reshape(16, 2, 64, VL), labels.reshape(1, BATCH), counts)
+    shapes = (
+        jax.ShapeDtypeStruct((8, 256, VL), BF),
+        jax.ShapeDtypeStruct((16, 512), BF),
+        jax.ShapeDtypeStruct((1,), F32),
+    )
+    smem = pl.BlockSpec(memory_space=pltpu.SMEM)
+    made = pl.pallas_call(
         kernel,
-        out_shape=(
-            jax.ShapeDtypeStruct((8, 256, VL), BF),
-            jax.ShapeDtypeStruct((16, 512), BF),
-            jax.ShapeDtypeStruct((1,), F32),
-        ),
+        out_shape=(v((8, 256, VL), BF), v((16, 512), BF), shapes[2]),
         in_specs=[hbm] * 4,
-        out_specs=(pl.BlockSpec(memory_space=pl.ANY), vmem, pl.BlockSpec(memory_space=pltpu.SMEM)),
+        out_specs=(vmem, vmem, smem),
         scratch_shapes=scratch,
         compiler_params=pltpu.CompilerParams(
-            collective_id=0, has_side_effects=True, vmem_limit_bytes=63 * 1024 * 1024
+            collective_id=0, has_side_effects=True, vmem_limit_bytes=50 * 1024 * 1024
         ),
         cost_estimate=pl.CostEstimate(flops=3 * 2**30, bytes_accessed=2**22, transcendentals=2**16),
-    )(hidden.T, weight.reshape(16, 2, 64, VL), labels.reshape(1, BATCH), counts)
+    )(*(pltpu.with_memory_space_constraint(a, pltpu.HBM) for a in args))
+    gw, gh, loss = pl.pallas_call(
+        hand_over,
+        out_shape=shapes,
+        in_specs=[vmem, vmem, hbm],
+        out_specs=(hbm,) * 3,
+        scratch_shapes=[pltpu.SMEM((1,), F32), dma((10,))],
+        compiler_params=pltpu.CompilerParams(vmem_limit_bytes=2**20),
+    )(*(pltpu.with_memory_space_constraint(a, m) for a, m in zip(made, (pltpu.VMEM, pltpu.VMEM, pltpu.HBM))))
     return gw.reshape(2048, VL), gh, loss
 
 

time: 104 us -> 95.8 us (0.921)
  local copies, waits for them, and re-layouts: 3.66 us -> 0 us
  Pallas kernels: 97.6 us -> 94.9 us
  between operations: 2.32 us -> 0.64 us
    unnamed x4 -> x0, local copies, waits for them, and re-layouts: 3.66 us -> none
    pallas_call x1 -> x2, Pallas kernels: 97.6 us -> 94.9 us  [the longest x1 92.9 us: body(): pl.pallas_call(kernel, out_shape=(v((8, 256, VL), BF), v((16, 512), BF),...]
where the time goes in v4:
time: 95.8 us; the launch traced here: 95.5 us
  Pallas kernels  94.9 us (99%)
    pallas_call x1, Pallas kernels, body(): pl.pallas_call(kernel, out_shape=(v((8, 256, VL), BF), v((16, 512), BF),...  92.9 us
    pallas_call x1, Pallas kernels, body(): pl.pallas_call(hand_over, out_shape=shapes, in_specs=[vmem, vmem, hbm], o...  2.04 us

profile of v4, /device:TPU:1, one launch (start us, length us, event | category | flops | bytes accessed | tf_op | source)
XLA Modules:
  0.0 95.5 jit_solution(7753572575936267986)
XLA Ops:
  0.6 92.9 %shard_map.67 = (bf16[8,256,512]{2,1,0:T(8,128)(2,1)S(1)}, bf16[16,512]{1,0:T(8,128)(2,1)S(1)}, f32[1]{0:T(128)}) custom-call(bf16[64,128]{1,0:T(8,128)(2,1)} %bitcast.6, bf16[16,2,64,512]{3,2,1,0:T(8,128)(2,1)} %bitcast.4, s32[1,128]{1,0:T(1,128)} %bitcast.7, s32[1,512]{1,0:T(1,128)} %cnt_hbm.1), custom_call_target="tpu_custom_call" | custom-call | flops 3221225472 | bytes 4194304 | tf_op jit(solution)/shard_map/pallas_call | solution.py:432
  93.5 2.0 %shard_map.68 = (bf16[8,256,512]{2,1,0:T(8,128)(2,1)}, bf16[16,512]{1,0:T(8,128)(2,1)}, f32[1]{0:T(128)}) custom-call(bf16[8,256,512]{2,1,0:T(8,128)(2,1)S(1)} %get-tuple-element.9.gw_in, bf16[16,512]{1,0:T(8,128)(2,1)S(1)} %get-tuple-element.10.gh_in, f32[1]{0:T(128)} %get-tuple-element.11.loss_in), custom_call_target="tpu_custom_call" | custom-call | tf_op jit(solution)/shard_map/pallas_call | solution.py:443

commit v5 on v4

--- a/solution.py
+++ b/solution.py
@@ -119,13 +119,14 @@
         copy.wait()
     pl.semaphore_wait(barrier, 25)
 
+    others = pl.ds(0, NZ - 1)
     halves = [pl.ds(0, FEAT // 2), pl.ds(FEAT // 2, FEAT // 2)]
 
     def start_z(h):
         def start(i, _):
             k = spread(i)
             ref = zbuf.at[z, halves[h]]
-            rcopy(ref, ref, az_s.at[h, k], az_r.at[h, k], to_z(zat(k))).start()
+            rcopy(ref, ref, az_s.at[h], az_r.at[h], to_z(zat(k))).start()
             return 0
 
         lax.fori_loop(0, NZ - 1, start, 0)
@@ -152,13 +153,8 @@
     fcol[...] = jnp.broadcast_to(factor, (BATCH, VL)).T
 
     def hid_x(_, h):
-        def wait_z(k, _):
-            ref = zbuf.at[z, halves[h]]
-            recv(zbuf.at[zat(-k), halves[h]], az_r.at[h, k])
-            rcopy(ref, ref, az_s.at[h, k], az_r.at[h, k], sibling).wait_send()
-            return 0
-
-        lax.fori_loop(1, NZ, wait_z, 0)
+        ref = zbuf.at[others, halves[h]]
+        recv(ref, az_r.at[h])
         for k in (2, 1, 3):
             to = xat(k)
             send(
@@ -252,16 +248,14 @@
 
     def start_sz(i, _):
         k = spread(i)
-        rcopy(stz.at[z], stz.at[z], sz_s.at[k], sz_r.at[k], to_z(zat(k))).start()
+        rcopy(stz.at[z], stz.at[z], sz_s, sz_r, to_z(zat(k))).start()
         return 0
 
-    def wait_sz(k, _):
-        recv(stz.at[zat(-k)], sz_r.at[k])
-        rcopy(stz.at[z], stz.at[z], sz_s.at[k], sz_r.at[k], sibling).wait_send()
-        return 0
-
     lax.fori_loop(0, NZ - 1, start_sz, 0)
-    lax.fori_loop(1, NZ, wait_sz, 0)
+    for h in (0, 1):
+        ref = zbuf.at[others, halves[h]]
+        rcopy(ref, ref, az_s.at[h], az_r.at[h], sibling).wait_send()
+    recv(stz.at[others], sz_r)
     me = y * 2 + c
     sty[me] = jnp.concatenate([*combine(stz), zero], axis=0)
     for k in range(1, 8):
@@ -332,7 +326,7 @@
         rz[zz] = (q[zz, :, y].astype(F32) + yl[k].astype(F32) + yr[k].astype(F32)).astype(BF)
         for j in range(0 if k else 1, ZL):
             l = lax.rem(zl0 + j, ZL)
-            send(rz.at[zz, l], zrb.at[z], fz_s.at[k, j], fz_r.at[z], to_z(ZL * zz + l))
+            send(rz.at[zz, l], zrb.at[z], fz_s.at[k, j], fz_r, to_z(ZL * zz + l))
 
     def gh_zd(k, h):
         zz = lax.rem(zs + k, NX)
@@ -342,7 +336,7 @@
         near = yl[k, two].astype(F32) + yr[k, two].astype(F32)
         rz[zz, two] = (q[zz, two, y].astype(F32) + near + y2[k, two].astype(F32)).astype(BF)
         for j in (2 * h, 2 * h + 1):
-            send(rz.at[zz, j], zrb.at[z], fz_s.at[k, j], fz_r.at[z], to_z(ZL * zz + j))
+            send(rz.at[zz, j], zrb.at[z], fz_s.at[k, j], fz_r, to_z(ZL * zz + j))
 
     def gw_tile(i):
         lhs = jnp.concatenate([ht[r, i // 2, i % 2].reshape(256, BATCH) for r in range(NX)], axis=1)
@@ -355,11 +349,8 @@
 
     zrb[z] = rz[zs, zl0]
 
-    def wait_fz(k, _):
-        recv(zrb.at[zat(-k)], fz_r.at[zat(-k)])
-        return 0
-
-    lax.fori_loop(1, NZ, wait_fz, 0)
+    rcopy(stz.at[others], stz.at[others], sz_s, sz_r, sibling).wait_send()
+    recv(zrb.at[others], fz_r)
     gh_out[...] = jnp.sum(zrb[...].astype(F32), axis=0).astype(BF)
 
     for d in sends:
@@ -415,10 +406,10 @@
         v((NX, ZL, 16, 512), BF),
         v((NZ, 16, 512), BF),
         dma, dma((3,)),
-        dma((2, 16)), dma((2, 16)), dma((2, 4)), dma((2, 4)), dma((4,)), dma((4,)), dma((4,)), dma((4,)),
+        dma((2,)), dma((2,)), dma((2, 4)), dma((2, 4)), dma((4,)), dma((4,)), dma((4,)), dma((4,)),
         dma((2, 4, 4)), dma((2, 4, 4)), dma((4,)), dma((4,)),
-        dma((6,)), dma((6,)), dma((16,)), dma((16,)), dma((8,)), dma((8,)), dma((4,)), dma((4,)), dma((4,)), dma((4,)),
-        dma((4,)), dma((4,)), dma((4, 6)), dma((4, 6)), dma((4, 4)), dma((16,)),
+        dma((6,)), dma((6,)), dma, dma, dma((8,)), dma((8,)), dma((4,)), dma((4,)), dma((4,)), dma((4,)),
+        dma((4,)), dma((4,)), dma((4, 6)), dma((4, 6)), dma((4, 4)), dma,
     ]
     vmem = pl.BlockSpec(memory_space=pltpu.VMEM)
     hbm = pl.BlockSpec(memory_space=pltpu.HBM)

time: 95.8 us -> 95.2 us (level)
  no operation moved by 1% of the time
where the time goes in v5:
time: 95.2 us; the launch traced here: 95 us
  Pallas kernels  94.4 us (99%)
    pallas_call x1, Pallas kernels, body(): pl.pallas_call(kernel, out_shape=(v((8, 256, VL), BF), v((16, 512), BF),...  92.3 us
    pallas_call x1, Pallas kernels, body(): pl.pallas_call(hand_over, out_shape=shapes, in_specs=[vmem, vmem, hbm], o...  2.04 us

profile of v5, /device:TPU:1, one launch (start us, length us, event | category | flops | bytes accessed | tf_op | source)
XLA Modules:
  0.0 95.0 jit_solution(18066367712638538255)
XLA Ops:
  0.6 92.3 %shard_map.67 = (bf16[8,256,512]{2,1,0:T(8,128)(2,1)S(1)}, bf16[16,512]{1,0:T(8,128)(2,1)S(1)}, f32[1]{0:T(128)}) custom-call(bf16[64,128]{1,0:T(8,128)(2,1)} %bitcast.6, bf16[16,2,64,512]{3,2,1,0:T(8,128)(2,1)} %bitcast.4, s32[1,128]{1,0:T(1,128)} %bitcast.7, s32[1,512]{1,0:T(1,128)} %cnt_hbm.1), custom_call_target="tpu_custom_call" | custom-call | flops 3221225472 | bytes 4194304 | tf_op jit(solution)/shard_map/pallas_call | solution.py:423
  93.0 2.0 %shard_map.68 = (bf16[8,256,512]{2,1,0:T(8,128)(2,1)}, bf16[16,512]{1,0:T(8,128)(2,1)}, f32[1]{0:T(128)}) custom-call(bf16[8,256,512]{2,1,0:T(8,128)(2,1)S(1)} %get-tuple-element.9.gw_in, bf16[16,512]{1,0:T(8,128)(2,1)S(1)} %get-tuple-element.10.gh_in, f32[1]{0:T(128)} %get-tuple-element.11.loss_in), custom_call_target="tpu_custom_call" | custom-call | tf_op jit(solution)/shard_map/pallas_call | solution.py:434

commit v6 on v5

--- a/solution.py
+++ b/solution.py
@@ -183,21 +183,21 @@
         r = xat(-k)
         recv(ht.at[r, :, oc], ac_r.at[k])
 
-        def tile(i, _):
-            rows = pl.ds(pl.multiple_of(i * 256, 256), 256)
+        top, low = pl.ds(0, 256), pl.ds(256, 256)
+
+        def tile(rows):
             part[r, rows] = jnp.dot(wt[rows, :], ht[r].reshape(2048, BATCH), preferred_element_type=F32)
-            return 0
-
-        lax.fori_loop(0, 2, tile, 0)
-        top, low = pl.ds(0, 256), pl.ds(256, 256)
+
+        tile(low if k == 3 else top)
         if k == 2:
             send(part.at[r, top], bufa, b_s.at[0], b_r.at[0], to_x(1))
-            send(part.at[r, low], bufb, b_s.at[1], b_r.at[1], to_x(-1))
         if k == 3:
             send(part.at[r, low], rfl.at[low], b_s.at[2], b_r.at[2], to_x(1))
         if k == 1:
             send(part.at[r, top], rfr.at[top], b_s.at[4], b_r.at[4], to_x(-1))
-
+        tile(top if k == 3 else low)
+        if k == 2:
+            send(part.at[r, low], bufb, b_s.at[1], b_r.at[1], to_x(-1))
     def logits_relay(k):
         r = xat(-k)
         top, low = pl.ds(0, 256), pl.ds(256, 256)

time: 95.2 us -> 95.5 us (level)
  no operation moved by 1% of the time
where the time goes in v6:
time: 95.5 us; the launch traced here: 95.3 us
  Pallas kernels  94.7 us (99%)
    pallas_call x1, Pallas kernels, body(): pl.pallas_call(kernel, out_shape=(v((8, 256, VL), BF), v((16, 512), BF),...  92.7 us
    pallas_call x1, Pallas kernels, body(): pl.pallas_call(hand_over, out_shape=shapes, in_specs=[vmem, vmem, hbm], o...  2.04 us

profile of v6, /device:TPU:1, one launch (start us, length us, event | category | flops | bytes accessed | tf_op | source)
XLA Modules:
  0.0 95.3 jit_solution(17542862655523652686)
XLA Ops:
  0.6 92.7 %shard_map.67 = (bf16[8,256,512]{2,1,0:T(8,128)(2,1)S(1)}, bf16[16,512]{1,0:T(8,128)(2,1)S(1)}, f32[1]{0:T(128)}) custom-call(bf16[64,128]{1,0:T(8,128)(2,1)} %bitcast.6, bf16[16,2,64,512]{3,2,1,0:T(8,128)(2,1)} %bitcast.4, s32[1,128]{1,0:T(1,128)} %bitcast.7, s32[1,512]{1,0:T(1,128)} %cnt_hbm.1), custom_call_target="tpu_custom_call" | custom-call | flops 3221225472 | bytes 4194304 | tf_op jit(solution)/shard_map/pallas_call | solution.py:423
  93.3 2.0 %shard_map.68 = (bf16[8,256,512]{2,1,0:T(8,128)(2,1)}, bf16[16,512]{1,0:T(8,128)(2,1)}, f32[1]{0:T(128)}) custom-call(bf16[8,256,512]{2,1,0:T(8,128)(2,1)S(1)} %get-tuple-element.9.gw_in, bf16[16,512]{1,0:T(8,128)(2,1)S(1)} %get-tuple-element.10.gh_in, f32[1]{0:T(128)} %get-tuple-element.11.loss_in), custom_call_target="tpu_custom_call" | custom-call | tf_op jit(solution)/shard_map/pallas_call | solution.py:434
